TPU v7x, 32 devices: a whole 2x2x4 slice. The times are simulated.
32 devices in a mesh: wide: 16 (over z, y, core), narrow: 2 (over x).
Axes of the slice: x: 2, y: 2, z: 4, core: 2. Of those that a mesh axis runs over, the one named last changes fastest.
Arguments:
- right_side: float32 [96, 128, 256], P(('wide', 'narrow')), may hold values from -6 to 6
- diag_inverse: float32 [96, 128, 128], P(('wide', 'narrow')), may hold values from -1 to 1, as said below
- off_tiles: float32 [96, 48, 128, 128], P('wide', 'narrow'), may hold values from -0.078125 to 0.078125
- tile_columns: int32 [96, 48], P('wide', 'narrow'), may hold values from 0 to 95, as said below
- colors: int32 [96], replicated, may hold values from 0 to 2, as said below
Outputs:
- potentials: float32 [96, 128, 256], P(('wide', 'narrow'))
Inputs may be any that keep to these rules, and one draw needn't show every extreme that they name: `colors`: each device along wide+narrow owns 3 consecutive blocks, exactly 1 of each color. `tile_columns`: slot k of a block row names a block owned by a device whose narrow index is k // 24, and of another color than the row's block. `diag_inverse`: symmetric tiles.
All inputs are finite; a program needn't handle non-finite values.
Results may differ from a plain program's by a relative error of at most 0.0001.
Values sent between devices are 32-bit elements; how exact they have to be, the bound alone decides.
A program may use at most 128 MiB of HBM per device.

v0:
```python
from functools import partial
import jax
import jax.numpy as jnp
from jax import lax
from jax.sharding import PartitionSpec as P


def block_terms(stack, tile_rows, column_slots, column_hues, start, count):
    picked = stack[column_hues, column_slots]
    return jnp.einsum("rkab,rkbl->ral", tile_rows, picked, precision=lax.Precision.HIGHEST)


def sweep(source, sorted_inv, sorted_tiles, slot_of, color_of, wide_size, narrow_size, per_color):
    label_width = source.shape[2]
    tile_size = source.shape[1]
    copies = jnp.zeros((3, wide_size * per_color, tile_size, label_width), jnp.float32)
    pieces = [None, None, None]
    for section, color_now in enumerate((0, 1, 2, 1, 0)):
        offset = color_now * per_color
        local_side = source[offset : offset + per_color]
        if section > 0:
            row_low = color_now * narrow_size * per_color
            row_high = row_low + narrow_size * per_color
            term_fn = partial(
                block_terms,
                copies,
                sorted_tiles[row_low:row_high],
                slot_of[row_low:row_high],
                color_of[row_low:row_high],
            )
            summed = lax.psum_scatter(
                term_fn(jnp.int32(0), lax.axis_size("narrow") * per_color),
                "narrow",
                scatter_dimension=0,
                tiled=True,
            )
            local_side = local_side - summed
        updated = jnp.einsum(
            "rab,rbl->ral",
            sorted_inv[offset : offset + per_color],
            local_side,
            precision=lax.Precision.HIGHEST,
        )
        pieces[color_now] = updated
        if section < 4:
            gathered = lax.all_gather(updated, "wide", axis=0, tiled=True)
            copies = copies.at[color_now].set(gathered)
    return jnp.concatenate(pieces, axis=0)


def shards(right_side, diag_inverse, off_tiles, tile_columns, colors):
    wide_size = lax.axis_size("wide")
    narrow_size = lax.axis_size("narrow")
    wide_at = lax.axis_index("wide")
    narrow_at = lax.axis_index("narrow")
    row_count = off_tiles.shape[0]
    own_count = right_side.shape[0]
    per_color = own_count // 3
    block_total = colors.shape[0]
    row_colors = lax.dynamic_slice_in_dim(colors, wide_at * row_count, row_count)
    row_order = jnp.argsort(row_colors, stable=True)
    sorted_tiles = off_tiles[row_order]
    sorted_cols = tile_columns[row_order]
    owner_colors = colors.reshape(block_total // own_count, own_count)
    owner_order = jnp.argsort(owner_colors, axis=1, stable=True)
    owner_inverse = jnp.argsort(owner_order, axis=1)
    ranks = (owner_inverse - owner_colors * per_color).reshape(block_total)
    block_ids = jnp.arange(block_total, dtype=jnp.int32)
    slot_all = block_ids // (narrow_size * own_count) * per_color + ranks
    slot_of = slot_all[sorted_cols]
    color_of = colors[sorted_cols]
    own_start = (wide_at * narrow_size + narrow_at) * own_count
    own_colors = lax.dynamic_slice_in_dim(colors, own_start, own_count)
    own_order = jnp.argsort(own_colors, stable=True)
    own_inverse = jnp.argsort(own_order)
    sorted_inv = diag_inverse[own_order]
    sorted_side = right_side[own_order]
    result = sweep(
        sorted_side, sorted_inv, sorted_tiles, slot_of, color_of, wide_size, narrow_size, per_color
    )
    return result[own_inverse]


def solution(mesh):
    return jax.shard_map(
        shards,
        mesh=mesh,
        in_specs=(
            P(("wide", "narrow"), None, None),
            P(("wide", "narrow"), None, None),
            P("wide", "narrow", None, None),
            P("wide", "narrow"),
            P(),
        ),
        out_specs=P(("wide", "narrow"), None, None),
        check_vma=False,
    )
```

profile of v0, /device:TPU:0, one launch (start us, length us, event | category | flops | bytes accessed | tf_op | source)
XLA Modules:
  0.0 317.8 jit_solution(14142655278700782819)
XLA Ops:
  6.5 0.8 dynamic_slice.6
  7.3 0.7 sort.85
  8.1 0.6 gather_fusion.1
  8.7 1.5 gather_fusion
  10.2 0.9 fusion.8
  11.2 0.8 reshape.195
  11.9 0.7 dynamic_slice.7
  12.7 1.0 sort.86
  13.7 1.2 gather_fusion.3
  15.1 0.6 sort.87
  15.8 0.6 sort.88
  16.4 0.1 copy.8
  16.5 0.1 reshape.196
  16.6 1.9 gather_fusion.4
  18.6 1.6 gather_fusion.5
  20.2 0.1 reshape.297
  20.3 0.1 reshape.295
  20.4 0.1 reshape.253
  20.5 8.6 %gather_fusion.2 = f32[6,24,128,128]{3,2,1,0:T(8,128)} fusion(f32[6,24,128,128]{3,2,1,0:T(8,128)} %param.15, s32[1024]{0:T(1024)S(1)} %pad_clamp_fusion.2), kind=kCustom, calls=%fused_computation.2 | custom fusion | bytes 18874392 | tf_op jit(solution)/shard_map/gather | solution.py:62
  29.1 26.3 %all-gather.9.cloned.1.call-done = f32[2048,256]{1,0:T(8,128)} async-done(((f32[128,256]{1,0:T(8,128)}), f32[2048,256]{1,0:T(8,128)}) %all-gather.9.cloned.1.call-update) | async-done | bytes 2097168 | tf_op jit(solution)/shard_map/all_gather | solution.py:46
  55.4 5.1 %scatter.14 = f32[3,16,128,256]{3,2,1,0:T(8,128)} pad(f32[1,16,128,256]{3,2,1,0:T(8,128)} %bitcast.69, f32[]{:T(128)} %constant.133.clone.1), padding=0_2x0_0x0_0x0_0 | pad | bytes 8388612 | tf_op jit(solution)/shard_map/scatter | solution.py:47
  60.4 6.5 %gather_fusion.6 = f32[48,128,256]{2,1,0:T(8,128)} fusion(f32[3,16,128,256]{3,2,1,0:T(8,128)} %scatter.14, s32[48]{0:T(128)S(1)} %reshape.253), kind=kCustom, calls=%fused_computation.6 | custom fusion | bytes 12583296 | tf_op jit(solution)/shard_map/gather | solution.py:9
  66.9 9.7 %convolution_bitcast_fusion.3 = f32[2,128,256]{2,1,0:T(8,128)} fusion(f32[6,24,128,128]{3,2,1,0:T(8,128)} %gather_fusion.2, f32[2,24,128,256]{3,2,1,0:T(8,128)} %bitcast.65), kind=kOutput, calls=%fused_computation.14 | convolution fusion | flops 2415919104 | bytes 15990784 | tf_op jit(solution)/shard_map/rkab,rkbl->ral/dot_general | solution.py:10
  76.7 10.5 %reduce-scatter.5.cloned.1.call-done = f32[1,128,256]{2,1,0:T(8,128)} async-done(((f32[2,128,256]{2,1,0:T(8,128)}), f32[1,128,256]{2,1,0:T(8,128)}) %reduce-scatter.5.cloned.1.call-update) | async-done | bytes 131088 | tf_op jit(solution)/shard_map/reduce_scatter | solution.py:31
  87.3 1.8 fusion.6
  89.3 0.1 reshape.259
  89.4 41.7 %all-gather.11.cloned.1.call-done = f32[2048,256]{1,0:T(8,128)} async-done(((f32[128,256]{1,0:T(8,128)}), f32[2048,256]{1,0:T(8,128)}) %all-gather.11.cloned.1.call-update) | async-done | bytes 2097168 | tf_op jit(solution)/shard_map/all_gather | solution.py:46
  131.1 3.2 %constant_dynamic-update-slice_fusion.2 = f32[3,16,128,256]{3,2,1,0:T(8,128)} fusion(f32[3,16,128,256]{3,2,1,0:T(8,128)} %scatter.14, f32[1,16,128,256]{3,2,1,0:T(8,128)} %bitcast.67), kind=kLoop, calls=%fused_computation.72 | loop fusion | bytes 4194304 | tf_op jit(solution)/shard_map/scatter | solution.py:47
  134.3 6.5 %gather_fusion.7 = f32[48,128,256]{2,1,0:T(8,128)} fusion(f32[3,16,128,256]{3,2,1,0:T(8,128)} %constant_dynamic-update-slice_fusion.2, s32[48]{0:T(128)S(1)} %reshape.259), kind=kCustom, calls=%fused_computation.7 | custom fusion | bytes 12583296 | tf_op jit(solution)/shard_map/gather | solution.py:9
  140.8 9.7 %convolution_bitcast_fusion.2 = f32[2,128,256]{2,1,0:T(8,128)} fusion(f32[6,24,128,128]{3,2,1,0:T(8,128)} %gather_fusion.2, f32[2,24,128,256]{3,2,1,0:T(8,128)} %bitcast.63), kind=kOutput, calls=%fused_computation.13 | convolution fusion | flops 2415919104 | bytes 15990784 | tf_op jit(solution)/shard_map/rkab,rkbl->ral/dot_general | solution.py:10
  150.6 10.5 %reduce-scatter.7.cloned.1.call-done = f32[1,128,256]{2,1,0:T(8,128)} async-done(((f32[2,128,256]{2,1,0:T(8,128)}), f32[1,128,256]{2,1,0:T(8,128)}) %reduce-scatter.7.cloned.1.call-update) | async-done | bytes 131088 | tf_op jit(solution)/shard_map/reduce_scatter | solution.py:31
  161.2 1.8 fusion.1
  163.0 0.2 reduce-scatter.9.cloned.1.call-start
  163.2 41.4 %all-gather.13.cloned.1.call-done = f32[2048,256]{1,0:T(8,128)} async-done(((f32[128,256]{1,0:T(8,128)}), f32[2048,256]{1,0:T(8,128)}) %all-gather.13.cloned.1.call-update) | async-done | bytes 2097168 | tf_op jit(solution)/shard_map/all_gather | solution.py:46
  204.6 3.1 constant_dynamic-update-slice_fusion.1
  207.7 6.5 %gather_fusion.8 = f32[48,128,256]{2,1,0:T(8,128)} fusion(f32[3,16,128,256]{3,2,1,0:T(8,128)} %constant_dynamic-update-slice_fusion.1, s32[48]{0:T(128)S(1)} %reshape.253), kind=kCustom, calls=%fused_computation.8 | custom fusion | bytes 12583296 | tf_op jit(solution)/shard_map/gather | solution.py:9
  214.2 9.7 %convolution_bitcast_fusion.1 = f32[2,128,256]{2,1,0:T(8,128)} fusion(f32[6,24,128,128]{3,2,1,0:T(8,128)} %gather_fusion.2, f32[2,24,128,256]{3,2,1,0:T(8,128)} %bitcast.64), kind=kOutput, calls=%fused_computation.12 | convolution fusion | flops 2415919104 | bytes 15990784 | tf_op jit(solution)/shard_map/rkab,rkbl->ral/dot_general | solution.py:10
  224.0 10.5 %reduce-scatter.9.cloned.1.call-done = f32[1,128,256]{2,1,0:T(8,128)} async-done(((f32[2,128,256]{2,1,0:T(8,128)}), f32[1,128,256]{2,1,0:T(8,128)}) %reduce-scatter.9.cloned.1.call-update) | async-done | bytes 131088 | tf_op jit(solution)/shard_map/reduce_scatter | solution.py:31
  234.5 1.8 fusion.4
  236.6 0.1 reshape.271
  236.7 41.7 %all-gather.15.cloned.1.call-done = f32[2048,256]{1,0:T(8,128)} async-done(((f32[128,256]{1,0:T(8,128)}), f32[2048,256]{1,0:T(8,128)}) %all-gather.15.cloned.1.call-update) | async-done | bytes 2097168 | tf_op jit(solution)/shard_map/all_gather | solution.py:46
  278.4 3.2 %constant_dynamic-update-slice_fusion = f32[3,16,128,256]{3,2,1,0:T(8,128)} fusion(f32[3,16,128,256]{3,2,1,0:T(8,128)} %constant_dynamic-update-slice_fusion.1, f32[1,16,128,256]{3,2,1,0:T(8,128)} %bitcast.66), kind=kLoop, calls=%fused_computation.70 | loop fusion | bytes 4194304 | tf_op jit(solution)/shard_map/scatter | solution.py:47
  281.6 6.5 %gather_fusion.9 = f32[48,128,256]{2,1,0:T(8,128)} fusion(f32[3,16,128,256]{3,2,1,0:T(8,128)} %constant_dynamic-update-slice_fusion, s32[48]{0:T(128)S(1)} %reshape.271), kind=kCustom, calls=%fused_computation.9 | custom fusion | bytes 12583296 | tf_op jit(solution)/shard_map/gather | solution.py:9
  288.1 9.8 %convolution_bitcast_fusion = f32[2,128,256]{2,1,0:T(8,128)} fusion(f32[6,24,128,128]{3,2,1,0:T(8,128)} %gather_fusion.2, f32[2,24,128,256]{3,2,1,0:T(8,128)} %bitcast.62), kind=kOutput, calls=%fused_computation.11 | convolution fusion | flops 2415919104 | bytes 15990784 | tf_op jit(solution)/shard_map/rkab,rkbl->ral/dot_general | solution.py:10
  297.9 0.7 sort.89
  298.6 9.8 %reduce-scatter.11.cloned.1.call-done = f32[1,128,256]{2,1,0:T(8,128)} async-done(((f32[2,128,256]{2,1,0:T(8,128)}), f32[1,128,256]{2,1,0:T(8,128)}) %reduce-scatter.11.cloned.1.call-update) | async-done | bytes 131088 | tf_op jit(solution)/shard_map/reduce_scatter | solution.py:31
  308.5 1.2 convolution_bitcast_fusion.4
  309.7 1.3 gather_fusion.10
  (48 shorter events, 1.2 us)
Async XLA Ops:
  6.5 1.6 copy-start
  6.5 48.8 %all-gather.9.cloned.1.call-start = ((), (), s32[]{:S(2)}) async-start(), calls=%async_computation.8 | async-start | bytes 2228224 | tf_op jit(solution)/shard_map/all_gather | solution.py:46
  11.1 76.2 %reduce-scatter.5.cloned.1.call-start = ((), (), s32[]{:S(2)}) async-start(), calls=%async_computation.4 | async-start | bytes 393216 | tf_op jit(solution)/shard_map/reduce_scatter | solution.py:31
  76.7 54.4 %all-gather.11.cloned.1.call-start = ((), (), s32[]{:S(2)}) async-start(), calls=%async_computation.9 | async-start | bytes 2228224 | tf_op jit(solution)/shard_map/all_gather | solution.py:46
  89.1 72.1 %reduce-scatter.7.cloned.1.call-start = ((), (), s32[]{:S(2)}) async-start(), calls=%async_computation.5 | async-start | bytes 393216 | tf_op jit(solution)/shard_map/reduce_scatter | solution.py:31
  150.6 54.0 %all-gather.13.cloned.1.call-start = ((), (), s32[]{:S(2)}) async-start(), calls=%async_computation.10 | async-start | bytes 2228224 | tf_op jit(solution)/shard_map/all_gather | solution.py:46
  163.0 71.5 %reduce-scatter.9.cloned.1.call-start = ((), (), s32[]{:S(2)}) async-start(), calls=%async_computation.6 | async-start | bytes 393216 | tf_op jit(solution)/shard_map/reduce_scatter | solution.py:31
  223.9 54.4 %all-gather.15.cloned.1.call-start = ((), (), s32[]{:S(2)}) async-start(), calls=%async_computation.11 | async-start | bytes 2228224 | tf_op jit(solution)/shard_map/all_gather | solution.py:46
  236.4 72.1 %reduce-scatter.11.cloned.1.call-start = ((), (), s32[]{:S(2)}) async-start(), calls=%async_computation.7 | async-start | bytes 393216 | tf_op jit(solution)/shard_map/reduce_scatter | solution.py:31
  288.1 21.6 %copy-start.1 = (f32[128,256]{1,0:T(8,128)S(1)}, f32[128,256]{1,0:T(8,128)}, u32[]{:S(2)}) copy-start(f32[128,256]{1,0:T(8,128)} %fusion.1) | copy-start | bytes 393220
  288.1 21.6 %copy-start.2 = (f32[128,256]{1,0:T(8,128)S(1)}, f32[128,256]{1,0:T(8,128)}, u32[]{:S(2)}) copy-start(f32[128,256]{1,0:T(8,128)} %fusion.4) | copy-start | bytes 393220
Sparse Core Ops, SparseCore 0:
  11.2 44.0 all-gather.8
  76.8 10.4 reduce-scatter.4
  89.7 41.4 all-gather.10
  150.7 10.4 reduce-scatter.6
  163.2 41.3 all-gather.12
  224.1 10.4 reduce-scatter.8
  236.9 41.4 all-gather.14
  298.0 10.4 reduce-scatter.10
where the time goes:
time: 318 us
  waiting for transfers between devices  193 us (61%)
  local copies, waits for them, and re-layouts  60.7 us (19%)
  matrix products  46.6 us (15%)
  between operations  13.6 us (4%)
  other arithmetic  3.94 us (1%)
    all_gather x4, waiting for transfers between devices, sweep(): gathered = lax.all_gather(updated, 'wide', axis=0, tiled=True)  151 us
    reduce_scatter x4, waiting for transfers between devices, sweep(): lax.psum_scatter(term_fn(jnp.int32(0), lax.axis_size('narrow') * per_colo...  41.4 us
    dot_general x4, matrix products, block_terms(): jnp.einsum('rkab,rkbl->ral', tile_rows, picked, precision=lax.Precision.H...  39 us
    gather x4, local copies, waits for them, and re-layouts, block_terms(): picked = stack[column_hues, column_slots]  26 us
    scatter x4, local copies, waits for them, and re-layouts, sweep(): copies = copies.at[color_now].set(gathered)  14.5 us
    gather x1, local copies, waits for them, and re-layouts, shards(): sorted_tiles = off_tiles[row_order]  8.58 us
    dot_general x5, matrix products, sweep(): jnp.einsum('rab,rbl->ral', sorted_inv[offset:offset + per_color], local_s...  7.55 us
  transfers between devices with their start and end apart: 8, of which 8 were waited for; matrix products, arithmetic and copies ran while one was open for 6% of the time, Pallas kernels for 0%

commit v1 on v0

--- a/solution.py
+++ b/solution.py
@@ -43,7 +43,27 @@
         )
         pieces[color_now] = updated
         if section < 4:
-            gathered = lax.all_gather(updated, "wide", axis=0, tiled=True)
+            ways, here, step = (lax.axis_size("wide"), lax.axis_index("wide"), updated.shape[0])
+            shape = [n * ways if d == 0 else n for d, n in enumerate(updated.shape)]
+            full = lax.dynamic_update_slice_in_dim(
+                jnp.zeros(shape, updated.dtype), updated, here * step, axis=0
+            )
+            going_up = going_down = updated
+            for far in range(1, ways // 2 + 1):
+                going_up = lax.ppermute(
+                    going_up, "wide", [(d, (d + 1) % ways) for d in range(ways)]
+                )
+                full = lax.dynamic_update_slice_in_dim(
+                    full, going_up, (here - far) % ways * step, axis=0
+                )
+                if 2 * far < ways:
+                    going_down = lax.ppermute(
+                        going_down, "wide", [(d, (d - 1) % ways) for d in range(ways)]
+                    )
+                    full = lax.dynamic_update_slice_in_dim(
+                        full, going_down, (here + far) % ways * step, axis=0
+                    )
+            gathered = full
             copies = copies.at[color_now].set(gathered)
     return jnp.concatenate(pieces, axis=0)
 

time: 318 us -> 373 us (1.17)
  starting transfers between devices: 0.48 us -> 127 us
  waiting for transfers between devices: 193 us -> 131 us
  matrix products: 46.6 us -> 41.2 us
  local copies, waits for them, and re-layouts: 60.7 us -> 55.5 us
    all_gather x4 -> x0, waiting for transfers between devices: 151 us -> none  [sweep(): gathered = lax.all_gather(updated, 'wide', axis=0, tiled=True)]
    ppermute x0 -> x60, starting transfers between devices: none -> 127 us  [the longest x28 126 us: sweep(): lax.ppermute(going_down, 'wide', [(d, (d - 1) % ways) for d in range(ways)])]
    ppermute x0 -> x60, waiting for transfers between devices: none -> 98.9 us  [the longest x32 98.7 us: sweep(): lax.ppermute(going_up, 'wide', [(d, (d + 1) % ways) for d in range(ways)])]
    reduce_scatter x4, waiting for transfers between devices: 41.4 us -> 31.9 us  [sweep(): lax.psum_scatter(term_fn(jnp.int32(0), lax.axis_size('narrow') * per_colo...]
    scatter x4, local copies, waits for them, and re-layouts: 14.5 us -> 8.05 us  [sweep(): copies = copies.at[color_now].set(gathered)]
    dot_general x5, matrix products: 7.55 us -> 2.2 us  [sweep(): jnp.einsum('rab,rbl->ral', sorted_inv[offset:offset + per_color], local_s...]
  transfers between devices with their start and end apart: 8 -> 64, of which waited for: 8 -> 36; matrix products, arithmetic and copies ran while one was open for 6% -> 5% of each run, Pallas kernels for 0% -> 0%
where the time goes in v1:
time: 373 us
  waiting for transfers between devices  131 us (35%)
  starting transfers between devices  127 us (34%)
  local copies, waits for them, and re-layouts  55.5 us (15%)
  matrix products  41.2 us (11%)
  between operations  13.8 us (4%)
  other arithmetic  3.86 us (1%)
    ppermute x28, starting transfers between devices, sweep(): lax.ppermute(going_down, 'wide', [(d, (d - 1) % ways) for d in range(ways)])  126 us
    ppermute x32, waiting for transfers between devices, sweep(): lax.ppermute(going_up, 'wide', [(d, (d + 1) % ways) for d in range(ways)])  98.7 us
    dot_general x4, matrix products, block_terms(): jnp.einsum('rkab,rkbl->ral', tile_rows, picked, precision=lax.Precision.H...  39 us
    reduce_scatter x4, waiting for transfers between devices, sweep(): lax.psum_scatter(term_fn(jnp.int32(0), lax.axis_size('narrow') * per_colo...  31.9 us
    gather x4, local copies, waits for them, and re-layouts, block_terms(): picked = stack[column_hues, column_slots]  26.1 us
    gather x1, local copies, waits for them, and re-layouts, shards(): sorted_tiles = off_tiles[row_order]  8.49 us
    scatter x4, local copies, waits for them, and re-layouts, sweep(): copies = copies.at[color_now].set(gathered)  8.05 us
  transfers between devices with their start and end apart: 64, of which 36 were waited for; matrix products, arithmetic and copies ran while one was open for 5% of the time, Pallas kernels for 0%

profile of v1, /device:TPU:0, one launch (start us, length us, event | category | flops | bytes accessed | tf_op | source)
XLA Modules:
  0.0 372.7 jit_solution(2985089520291559216)
XLA Ops:
  11.2 5.1 %collective-permute-start.1 = (f32[1,128,256]{2,1,0:T(8,128)S(1)}, f32[1,128,256]{2,1,0:T(8,128)S(1)}, u32[]{:S(2)}, u32[]{:S(2)}) collective-permute-start(f32[1,128,256]{2,1,0:T(8,128)S(1)} %bitcast.215), channel_id=1, source_target_pairs={{0,30},{2,0},{4,2},{6,4},{8,6},{10,8},{12,10},{14,12},{16,14},{18,... | collective-permute-start | bytes 393224 | tf_op jit(solution)/shard_map/ppermute | solution.py:60
  23.2 8.5 %gather_fusion.2 = f32[6,24,128,128]{3,2,1,0:T(8,128)} fusion(f32[6,24,128,128]{3,2,1,0:T(8,128)} %param.15, s32[1024]{0:T(1024)S(1)} %pad_clamp_fusion.2), kind=kCustom, calls=%fused_computation.2 | custom fusion | bytes 18874392 | tf_op jit(solution)/shard_map/gather | solution.py:82
  31.7 4.4 %collective-permute-start.3 = (f32[1,128,256]{2,1,0:T(8,128)S(1)}, f32[1,128,256]{2,1,0:T(8,128)S(1)}, u32[]{:S(2)}, u32[]{:S(2)}) collective-permute-start(f32[1,128,256]{2,1,0:T(8,128)S(1)} %collective-permute-done.1), channel_id=1, source_target_pairs={{0,30},{2,0},{4,2},{6,4},{8,6},{10,8},{12,10},{14,12},{16,14},{18,... | collective-permute-start | bytes 393224 | tf_op jit(solution)/shard_map/ppermute | solution.py:60
  38.8 4.5 %collective-permute-start.5 = (f32[1,128,256]{2,1,0:T(8,128)S(1)}, f32[1,128,256]{2,1,0:T(8,128)S(1)}, u32[]{:S(2)}, u32[]{:S(2)}) collective-permute-start(f32[1,128,256]{2,1,0:T(8,128)S(1)} %collective-permute-done.3), channel_id=1, source_target_pairs={{0,30},{2,0},{4,2},{6,4},{8,6},{10,8},{12,10},{14,12},{16,14},{18,... | collective-permute-start | bytes 393224 | tf_op jit(solution)/shard_map/ppermute | solution.py:60
  46.0 4.4 %collective-permute-start.7 = (f32[1,128,256]{2,1,0:T(8,128)S(1)}, f32[1,128,256]{2,1,0:T(8,128)S(1)}, u32[]{:S(2)}, u32[]{:S(2)}) collective-permute-start(f32[1,128,256]{2,1,0:T(8,128)S(1)} %collective-permute-done.5), channel_id=1, source_target_pairs={{0,30},{2,0},{4,2},{6,4},{8,6},{10,8},{12,10},{14,12},{16,14},{18,... | collective-permute-start | bytes 393224 | tf_op jit(solution)/shard_map/ppermute | solution.py:60
  50.5 2.7 collective-permute-done.6
  53.2 4.4 %collective-permute-start.9 = (f32[1,128,256]{2,1,0:T(8,128)S(1)}, f32[1,128,256]{2,1,0:T(8,128)S(1)}, u32[]{:S(2)}, u32[]{:S(2)}) collective-permute-start(f32[1,128,256]{2,1,0:T(8,128)S(1)} %collective-permute-done.7), channel_id=1, source_target_pairs={{0,30},{2,0},{4,2},{6,4},{8,6},{10,8},{12,10},{14,12},{16,14},{18,... | collective-permute-start | bytes 393224 | tf_op jit(solution)/shard_map/ppermute | solution.py:60
  60.4 4.4 %collective-permute-start.11 = (f32[1,128,256]{2,1,0:T(8,128)S(1)}, f32[1,128,256]{2,1,0:T(8,128)S(1)}, u32[]{:S(2)}, u32[]{:S(2)}) collective-permute-start(f32[1,128,256]{2,1,0:T(8,128)S(1)} %collective-permute-done.9), channel_id=1, source_target_pairs={{0,30},{2,0},{4,2},{6,4},{8,6},{10,8},{12,10},{14,12},{16,14},{18,... | collective-permute-start | bytes 393224 | tf_op jit(solution)/shard_map/ppermute | solution.py:60
  67.6 4.4 %collective-permute-start.13 = (f32[1,128,256]{2,1,0:T(8,128)S(1)}, f32[1,128,256]{2,1,0:T(8,128)S(1)}, u32[]{:S(2)}, u32[]{:S(2)}) collective-permute-start(f32[1,128,256]{2,1,0:T(8,128)S(1)} %collective-permute-done.11), channel_id=1, source_target_pairs={{0,30},{2,0},{4,2},{6,4},{8,6},{10,8},{12,10},{14,12},{16,14},{18,... | collective-permute-start | bytes 393224 | tf_op jit(solution)/shard_map/ppermute | solution.py:60
  74.7 7.0 %collective-permute-done.14 = f32[1,128,256]{2,1,0:T(8,128)S(1)} collective-permute-done((f32[1,128,256]{2,1,0:T(8,128)S(1)}, f32[1,128,256]{2,1,0:T(8,128)S(1)}, u32[]{:S(2)}, u32[]{:S(2)}) %collective-permute-start.14) | collective-permute-done | bytes 131104 | tf_op jit(solution)/shard_map/ppermute | solution.py:53
  81.8 3.3 scatter.14
  85.1 6.5 %gather_fusion.6 = f32[48,128,256]{2,1,0:T(8,128)} fusion(f32[3,16,128,256]{3,2,1,0:T(8,128)} %scatter.14, s32[48]{0:T(128)S(1)} %reshape.936), kind=kCustom, calls=%fused_computation.6 | custom fusion | bytes 12583296 | tf_op jit(solution)/shard_map/gather | solution.py:9
  91.6 9.7 %convolution_bitcast_fusion.3 = f32[2,128,256]{2,1,0:T(8,128)} fusion(f32[6,24,128,128]{3,2,1,0:T(8,128)} %gather_fusion.2, f32[2,24,128,256]{3,2,1,0:T(8,128)} %bitcast.207), kind=kOutput, calls=%fused_computation.14 | convolution fusion | flops 2415919104 | bytes 15990784 | tf_op jit(solution)/shard_map/rkab,rkbl->ral/dot_general | solution.py:10
  101.6 9.3 %reduce-scatter.5.cloned.1.call-done = f32[1,128,256]{2,1,0:T(8,128)} async-done(((f32[2,128,256]{2,1,0:T(8,128)}), f32[1,128,256]{2,1,0:T(8,128)}) %reduce-scatter.5.cloned.1.call-update) | async-done | bytes 131088 | tf_op jit(solution)/shard_map/reduce_scatter | solution.py:31
  112.2 4.4 %collective-permute-start.16 = (f32[1,128,256]{2,1,0:T(8,128)S(1)}, f32[1,128,256]{2,1,0:T(8,128)S(1)}, u32[]{:S(2)}, u32[]{:S(2)}) collective-permute-start(f32[1,128,256]{2,1,0:T(8,128)S(1)} %bitcast.217), channel_id=1, source_target_pairs={{0,30},{2,0},{4,2},{6,4},{8,6},{10,8},{12,10},{14,12},{16,14},{18,... | collective-permute-start | bytes 393224 | tf_op jit(solution)/shard_map/ppermute | solution.py:60
  119.3 4.5 %collective-permute-start.18 = (f32[1,128,256]{2,1,0:T(8,128)S(1)}, f32[1,128,256]{2,1,0:T(8,128)S(1)}, u32[]{:S(2)}, u32[]{:S(2)}) collective-permute-start(f32[1,128,256]{2,1,0:T(8,128)S(1)} %collective-permute-done.16), channel_id=1, source_target_pairs={{0,30},{2,0},{4,2},{6,4},{8,6},{10,8},{12,10},{14,12},{16,14},{18,... | collective-permute-start | bytes 393224 | tf_op jit(solution)/shard_map/ppermute | solution.py:60
  126.4 4.5 %collective-permute-start.20 = (f32[1,128,256]{2,1,0:T(8,128)S(1)}, f32[1,128,256]{2,1,0:T(8,128)S(1)}, u32[]{:S(2)}, u32[]{:S(2)}) collective-permute-start(f32[1,128,256]{2,1,0:T(8,128)S(1)} %collective-permute-done.18), channel_id=1, source_target_pairs={{0,30},{2,0},{4,2},{6,4},{8,6},{10,8},{12,10},{14,12},{16,14},{18,... | collective-permute-start | bytes 393224 | tf_op jit(solution)/shard_map/ppermute | solution.py:60
  133.6 4.5 %collective-permute-start.22 = (f32[1,128,256]{2,1,0:T(8,128)S(1)}, f32[1,128,256]{2,1,0:T(8,128)S(1)}, u32[]{:S(2)}, u32[]{:S(2)}) collective-permute-start(f32[1,128,256]{2,1,0:T(8,128)S(1)} %collective-permute-done.20), channel_id=1, source_target_pairs={{0,30},{2,0},{4,2},{6,4},{8,6},{10,8},{12,10},{14,12},{16,14},{18,... | collective-permute-start | bytes 393224 | tf_op jit(solution)/shard_map/ppermute | solution.py:60
  140.8 4.5 %collective-permute-start.24 = (f32[1,128,256]{2,1,0:T(8,128)S(1)}, f32[1,128,256]{2,1,0:T(8,128)S(1)}, u32[]{:S(2)}, u32[]{:S(2)}) collective-permute-start(f32[1,128,256]{2,1,0:T(8,128)S(1)} %collective-permute-done.22), channel_id=1, source_target_pairs={{0,30},{2,0},{4,2},{6,4},{8,6},{10,8},{12,10},{14,12},{16,14},{18,... | collective-permute-start | bytes 393224 | tf_op jit(solution)/shard_map/ppermute | solution.py:60
  148.0 4.5 %collective-permute-start.26 = (f32[1,128,256]{2,1,0:T(8,128)S(1)}, f32[1,128,256]{2,1,0:T(8,128)S(1)}, u32[]{:S(2)}, u32[]{:S(2)}) collective-permute-start(f32[1,128,256]{2,1,0:T(8,128)S(1)} %collective-permute-done.24), channel_id=1, source_target_pairs={{0,30},{2,0},{4,2},{6,4},{8,6},{10,8},{12,10},{14,12},{16,14},{18,... | collective-permute-start | bytes 393224 | tf_op jit(solution)/shard_map/ppermute | solution.py:60
  155.2 4.5 %collective-permute-start.28 = (f32[1,128,256]{2,1,0:T(8,128)S(1)}, f32[1,128,256]{2,1,0:T(8,128)S(1)}, u32[]{:S(2)}, u32[]{:S(2)}) collective-permute-start(f32[1,128,256]{2,1,0:T(8,128)S(1)} %collective-permute-done.26), channel_id=1, source_target_pairs={{0,30},{2,0},{4,2},{6,4},{8,6},{10,8},{12,10},{14,12},{16,14},{18,... | collective-permute-start | bytes 393224 | tf_op jit(solution)/shard_map/ppermute | solution.py:60
  162.3 7.0 %collective-permute-done.29 = f32[1,128,256]{2,1,0:T(8,128)S(1)} collective-permute-done((f32[1,128,256]{2,1,0:T(8,128)S(1)}, f32[1,128,256]{2,1,0:T(8,128)S(1)}, u32[]{:S(2)}, u32[]{:S(2)}) %collective-permute-start.29) | collective-permute-done | bytes 131104 | tf_op jit(solution)/shard_map/ppermute | solution.py:53
  171.0 6.5 %gather_fusion.7 = f32[48,128,256]{2,1,0:T(8,128)} fusion(f32[3,16,128,256]{3,2,1,0:T(8,128)} %constant_dynamic-update-slice_fusion.2, s32[48]{0:T(128)S(1)} %reshape.942), kind=kCustom, calls=%fused_computation.7 | custom fusion | bytes 12583296 | tf_op jit(solution)/shard_map/gather | solution.py:9
  177.5 9.7 %convolution_bitcast_fusion.2 = f32[2,128,256]{2,1,0:T(8,128)} fusion(f32[6,24,128,128]{3,2,1,0:T(8,128)} %gather_fusion.2, f32[2,24,128,256]{3,2,1,0:T(8,128)} %bitcast.205), kind=kOutput, calls=%fused_computation.13 | convolution fusion | flops 2415919104 | bytes 15990784 | tf_op jit(solution)/shard_map/rkab,rkbl->ral/dot_general | solution.py:10
  187.3 7.8 %reduce-scatter.7.cloned.1.call-done = f32[1,128,256]{2,1,0:T(8,128)} async-done(((f32[2,128,256]{2,1,0:T(8,128)}), f32[1,128,256]{2,1,0:T(8,128)}) %reduce-scatter.7.cloned.1.call-update) | async-done | bytes 131088 | tf_op jit(solution)/shard_map/reduce_scatter | solution.py:31
  196.4 4.4 %collective-permute-start.31 = (f32[1,128,256]{2,1,0:T(8,128)S(1)}, f32[1,128,256]{2,1,0:T(8,128)S(1)}, u32[]{:S(2)}, u32[]{:S(2)}) collective-permute-start(f32[1,128,256]{2,1,0:T(8,128)S(1)} %bitcast.209), channel_id=1, source_target_pairs={{0,30},{2,0},{4,2},{6,4},{8,6},{10,8},{12,10},{14,12},{16,14},{18,... | collective-permute-start | bytes 393224 | tf_op jit(solution)/shard_map/ppermute | solution.py:60
  200.8 2.8 collective-permute-done.30
  203.6 4.5 %collective-permute-start.33 = (f32[1,128,256]{2,1,0:T(8,128)S(1)}, f32[1,128,256]{2,1,0:T(8,128)S(1)}, u32[]{:S(2)}, u32[]{:S(2)}) collective-permute-start(f32[1,128,256]{2,1,0:T(8,128)S(1)} %collective-permute-done.31), channel_id=1, source_target_pairs={{0,30},{2,0},{4,2},{6,4},{8,6},{10,8},{12,10},{14,12},{16,14},{18,... | collective-permute-start | bytes 393224 | tf_op jit(solution)/shard_map/ppermute | solution.py:60
  210.7 4.5 %collective-permute-start.35 = (f32[1,128,256]{2,1,0:T(8,128)S(1)}, f32[1,128,256]{2,1,0:T(8,128)S(1)}, u32[]{:S(2)}, u32[]{:S(2)}) collective-permute-start(f32[1,128,256]{2,1,0:T(8,128)S(1)} %collective-permute-done.33), channel_id=1, source_target_pairs={{0,30},{2,0},{4,2},{6,4},{8,6},{10,8},{12,10},{14,12},{16,14},{18,... | collective-permute-start | bytes 393224 | tf_op jit(solution)/shard_map/ppermute | solution.py:60
  217.9 4.5 %collective-permute-start.37 = (f32[1,128,256]{2,1,0:T(8,128)S(1)}, f32[1,128,256]{2,1,0:T(8,128)S(1)}, u32[]{:S(2)}, u32[]{:S(2)}) collective-permute-start(f32[1,128,256]{2,1,0:T(8,128)S(1)} %collective-permute-done.35), channel_id=1, source_target_pairs={{0,30},{2,0},{4,2},{6,4},{8,6},{10,8},{12,10},{14,12},{16,14},{18,... | collective-permute-start | bytes 393224 | tf_op jit(solution)/shard_map/ppermute | solution.py:60
  225.1 4.5 %collective-permute-start.39 = (f32[1,128,256]{2,1,0:T(8,128)S(1)}, f32[1,128,256]{2,1,0:T(8,128)S(1)}, u32[]{:S(2)}, u32[]{:S(2)}) collective-permute-start(f32[1,128,256]{2,1,0:T(8,128)S(1)} %collective-permute-done.37), channel_id=1, source_target_pairs={{0,30},{2,0},{4,2},{6,4},{8,6},{10,8},{12,10},{14,12},{16,14},{18,... | collective-permute-start | bytes 393224 | tf_op jit(solution)/shard_map/ppermute | solution.py:60
  232.3 4.5 %collective-permute-start.41 = (f32[1,128,256]{2,1,0:T(8,128)S(1)}, f32[1,128,256]{2,1,0:T(8,128)S(1)}, u32[]{:S(2)}, u32[]{:S(2)}) collective-permute-start(f32[1,128,256]{2,1,0:T(8,128)S(1)} %collective-permute-done.39), channel_id=1, source_target_pairs={{0,30},{2,0},{4,2},{6,4},{8,6},{10,8},{12,10},{14,12},{16,14},{18,... | collective-permute-start | bytes 393224 | tf_op jit(solution)/shard_map/ppermute | solution.py:60
  239.5 4.5 %collective-permute-start.43 = (f32[1,128,256]{2,1,0:T(8,128)S(1)}, f32[1,128,256]{2,1,0:T(8,128)S(1)}, u32[]{:S(2)}, u32[]{:S(2)}) collective-permute-start(f32[1,128,256]{2,1,0:T(8,128)S(1)} %collective-permute-done.41), channel_id=1, source_target_pairs={{0,30},{2,0},{4,2},{6,4},{8,6},{10,8},{12,10},{14,12},{16,14},{18,... | collective-permute-start | bytes 393224 | tf_op jit(solution)/shard_map/ppermute | solution.py:60
  246.6 7.0 %collective-permute-done.44 = f32[1,128,256]{2,1,0:T(8,128)S(1)} collective-permute-done((f32[1,128,256]{2,1,0:T(8,128)S(1)}, f32[1,128,256]{2,1,0:T(8,128)S(1)}, u32[]{:S(2)}, u32[]{:S(2)}) %collective-permute-start.44) | collective-permute-done | bytes 131104 | tf_op jit(solution)/shard_map/ppermute | solution.py:53
  255.1 6.5 %gather_fusion.8 = f32[48,128,256]{2,1,0:T(8,128)} fusion(f32[3,16,128,256]{3,2,1,0:T(8,128)} %constant_dynamic-update-slice_fusion.1, s32[48]{0:T(128)S(1)} %reshape.936), kind=kCustom, calls=%fused_computation.8 | custom fusion | bytes 12583296 | tf_op jit(solution)/shard_map/gather | solution.py:9
  261.6 9.7 %convolution_bitcast_fusion.1 = f32[2,128,256]{2,1,0:T(8,128)} fusion(f32[6,24,128,128]{3,2,1,0:T(8,128)} %gather_fusion.2, f32[2,24,128,256]{3,2,1,0:T(8,128)} %bitcast.206), kind=kOutput, calls=%fused_computation.12 | convolution fusion | flops 2415919104 | bytes 15990784 | tf_op jit(solution)/shard_map/rkab,rkbl->ral/dot_general | solution.py:10
  271.6 7.7 %reduce-scatter.9.cloned.1.call-done = f32[1,128,256]{2,1,0:T(8,128)} async-done(((f32[2,128,256]{2,1,0:T(8,128)}), f32[1,128,256]{2,1,0:T(8,128)}) %reduce-scatter.9.cloned.1.call-update) | async-done | bytes 131088 | tf_op jit(solution)/shard_map/reduce_scatter | solution.py:31
  280.6 4.4 %collective-permute-start.46 = (f32[1,128,256]{2,1,0:T(8,128)S(1)}, f32[1,128,256]{2,1,0:T(8,128)S(1)}, u32[]{:S(2)}, u32[]{:S(2)}) collective-permute-start(f32[1,128,256]{2,1,0:T(8,128)S(1)} %bitcast.212), channel_id=1, source_target_pairs={{0,30},{2,0},{4,2},{6,4},{8,6},{10,8},{12,10},{14,12},{16,14},{18,... | collective-permute-start | bytes 393224 | tf_op jit(solution)/shard_map/ppermute | solution.py:60
  287.8 4.5 %collective-permute-start.48 = (f32[1,128,256]{2,1,0:T(8,128)S(1)}, f32[1,128,256]{2,1,0:T(8,128)S(1)}, u32[]{:S(2)}, u32[]{:S(2)}) collective-permute-start(f32[1,128,256]{2,1,0:T(8,128)S(1)} %collective-permute-done.46), channel_id=1, source_target_pairs={{0,30},{2,0},{4,2},{6,4},{8,6},{10,8},{12,10},{14,12},{16,14},{18,... | collective-permute-start | bytes 393224 | tf_op jit(solution)/shard_map/ppermute | solution.py:60
  294.9 4.5 %collective-permute-start.50 = (f32[1,128,256]{2,1,0:T(8,128)S(1)}, f32[1,128,256]{2,1,0:T(8,128)S(1)}, u32[]{:S(2)}, u32[]{:S(2)}) collective-permute-start(f32[1,128,256]{2,1,0:T(8,128)S(1)} %collective-permute-done.48), channel_id=1, source_target_pairs={{0,30},{2,0},{4,2},{6,4},{8,6},{10,8},{12,10},{14,12},{16,14},{18,... | collective-permute-start | bytes 393224 | tf_op jit(solution)/shard_map/ppermute | solution.py:60
  302.1 4.5 %collective-permute-start.52 = (f32[1,128,256]{2,1,0:T(8,128)S(1)}, f32[1,128,256]{2,1,0:T(8,128)S(1)}, u32[]{:S(2)}, u32[]{:S(2)}) collective-permute-start(f32[1,128,256]{2,1,0:T(8,128)S(1)} %collective-permute-done.50), channel_id=1, source_target_pairs={{0,30},{2,0},{4,2},{6,4},{8,6},{10,8},{12,10},{14,12},{16,14},{18,... | collective-permute-start | bytes 393224 | tf_op jit(solution)/shard_map/ppermute | solution.py:60
  309.2 4.5 %collective-permute-start.54 = (f32[1,128,256]{2,1,0:T(8,128)S(1)}, f32[1,128,256]{2,1,0:T(8,128)S(1)}, u32[]{:S(2)}, u32[]{:S(2)}) collective-permute-start(f32[1,128,256]{2,1,0:T(8,128)S(1)} %collective-permute-done.52), channel_id=1, source_target_pairs={{0,30},{2,0},{4,2},{6,4},{8,6},{10,8},{12,10},{14,12},{16,14},{18,... | collective-permute-start | bytes 393224 | tf_op jit(solution)/shard_map/ppermute | solution.py:60
  316.4 4.7 %collective-permute-start.56 = (f32[1,128,256]{2,1,0:T(8,128)S(1)}, f32[1,128,256]{2,1,0:T(8,128)S(1)}, u32[]{:S(2)}, u32[]{:S(2)}) collective-permute-start(f32[1,128,256]{2,1,0:T(8,128)S(1)} %collective-permute-done.54), channel_id=1, source_target_pairs={{0,30},{2,0},{4,2},{6,4},{8,6},{10,8},{12,10},{14,12},{16,14},{18,... | collective-permute-start | bytes 393224 | tf_op jit(solution)/shard_map/ppermute | solution.py:60
  323.7 4.7 %collective-permute-start.58 = (f32[1,128,256]{2,1,0:T(8,128)S(1)}, f32[1,128,256]{2,1,0:T(8,128)S(1)}, u32[]{:S(2)}, u32[]{:S(2)}) collective-permute-start(f32[1,128,256]{2,1,0:T(8,128)S(1)} %collective-permute-done.56), channel_id=1, source_target_pairs={{0,30},{2,0},{4,2},{6,4},{8,6},{10,8},{12,10},{14,12},{16,14},{18,... | collective-permute-start | bytes 393224 | tf_op jit(solution)/shard_map/ppermute | solution.py:60
  330.9 6.9 %collective-permute-done.59 = f32[1,128,256]{2,1,0:T(8,128)S(1)} collective-permute-done((f32[1,128,256]{2,1,0:T(8,128)S(1)}, f32[1,128,256]{2,1,0:T(8,128)S(1)}, u32[]{:S(2)}, u32[]{:S(2)}) %collective-permute-start.59) | collective-permute-done | bytes 131104 | tf_op jit(solution)/shard_map/ppermute | solution.py:53
  339.4 6.5 %gather_fusion.9 = f32[48,128,256]{2,1,0:T(8,128)} fusion(f32[3,16,128,256]{3,2,1,0:T(8,128)} %constant_dynamic-update-slice_fusion, s32[48]{0:T(128)S(1)} %reshape.954), kind=kCustom, calls=%fused_computation.9 | custom fusion | bytes 12583296 | tf_op jit(solution)/shard_map/gather | solution.py:9
  345.9 9.8 %convolution_bitcast_fusion = f32[2,128,256]{2,1,0:T(8,128)} fusion(f32[6,24,128,128]{3,2,1,0:T(8,128)} %gather_fusion.2, f32[2,24,128,256]{3,2,1,0:T(8,128)} %bitcast.204), kind=kOutput, calls=%fused_computation.11 | convolution fusion | flops 2415919104 | bytes 15990784 | tf_op jit(solution)/shard_map/rkab,rkbl->ral/dot_general | solution.py:10
  356.5 7.1 %reduce-scatter.11.cloned.1.call-done = f32[1,128,256]{2,1,0:T(8,128)} async-done(((f32[2,128,256]{2,1,0:T(8,128)}), f32[1,128,256]{2,1,0:T(8,128)}) %reduce-scatter.11.cloned.1.call-update) | async-done | bytes 131088 | tf_op jit(solution)/shard_map/reduce_scatter | solution.py:31
  (228 shorter events, 90.1 us)
Async XLA Ops:
  6.5 104.3 %reduce-scatter.5.cloned.1.call-start = ((), (), s32[]{:S(2)}) async-start(), calls=%async_computation.4 | async-start | bytes 393216 | tf_op jit(solution)/shard_map/reduce_scatter | solution.py:31
  10.7 21.0 %collective-permute-start = (f32[1,128,256]{2,1,0:T(8,128)S(1)}, f32[1,128,256]{2,1,0:T(8,128)S(1)}, u32[]{:S(2)}, u32[]{:S(2)}) collective-permute-start(f32[1,128,256]{2,1,0:T(8,128)S(1)} %bitcast.214), channel_id=1, source_target_pairs={{0,2},{2,4},{4,6},{6,8},{8,10},{10,12},{12,14},{14,16},{16,18},{18... | collective-permute-start | bytes 393224 | tf_op jit(solution)/shard_map/ppermute | solution.py:53
  11.2 20.5 %collective-permute-start.1 = (f32[1,128,256]{2,1,0:T(8,128)S(1)}, f32[1,128,256]{2,1,0:T(8,128)S(1)}, u32[]{:S(2)}, u32[]{:S(2)}) collective-permute-start(f32[1,128,256]{2,1,0:T(8,128)S(1)} %bitcast.215), channel_id=1, source_target_pairs={{0,30},{2,0},{4,2},{6,4},{8,6},{10,8},{12,10},{14,12},{16,14},{18,... | collective-permute-start | bytes 393224 | tf_op jit(solution)/shard_map/ppermute | solution.py:60
  31.7 7.1 %collective-permute-start.2 = (f32[1,128,256]{2,1,0:T(8,128)S(1)}, f32[1,128,256]{2,1,0:T(8,128)S(1)}, u32[]{:S(2)}, u32[]{:S(2)}) collective-permute-start(f32[1,128,256]{2,1,0:T(8,128)S(1)} %collective-permute-done), channel_id=1, source_target_pairs={{0,2},{2,4},{4,6},{6,8},{8,10},{10,12},{12,14},{14,16},{16,18},{18... | collective-permute-start | bytes 393224 | tf_op jit(solution)/shard_map/ppermute | solution.py:53
  31.7 7.1 %collective-permute-start.3 = (f32[1,128,256]{2,1,0:T(8,128)S(1)}, f32[1,128,256]{2,1,0:T(8,128)S(1)}, u32[]{:S(2)}, u32[]{:S(2)}) collective-permute-start(f32[1,128,256]{2,1,0:T(8,128)S(1)} %collective-permute-done.1), channel_id=1, source_target_pairs={{0,30},{2,0},{4,2},{6,4},{8,6},{10,8},{12,10},{14,12},{16,14},{18,... | collective-permute-start | bytes 393224 | tf_op jit(solution)/shard_map/ppermute | solution.py:60
  38.8 7.2 %collective-permute-start.4 = (f32[1,128,256]{2,1,0:T(8,128)S(1)}, f32[1,128,256]{2,1,0:T(8,128)S(1)}, u32[]{:S(2)}, u32[]{:S(2)}) collective-permute-start(f32[1,128,256]{2,1,0:T(8,128)S(1)} %collective-permute-done.2), channel_id=1, source_target_pairs={{0,2},{2,4},{4,6},{6,8},{8,10},{10,12},{12,14},{14,16},{16,18},{18... | collective-permute-start | bytes 393224 | tf_op jit(solution)/shard_map/ppermute | solution.py:53
  38.8 7.2 %collective-permute-start.5 = (f32[1,128,256]{2,1,0:T(8,128)S(1)}, f32[1,128,256]{2,1,0:T(8,128)S(1)}, u32[]{:S(2)}, u32[]{:S(2)}) collective-permute-start(f32[1,128,256]{2,1,0:T(8,128)S(1)} %collective-permute-done.3), channel_id=1, source_target_pairs={{0,30},{2,0},{4,2},{6,4},{8,6},{10,8},{12,10},{14,12},{16,14},{18,... | collective-permute-start | bytes 393224 | tf_op jit(solution)/shard_map/ppermute | solution.py:60
  46.0 7.2 %collective-permute-start.6 = (f32[1,128,256]{2,1,0:T(8,128)S(1)}, f32[1,128,256]{2,1,0:T(8,128)S(1)}, u32[]{:S(2)}, u32[]{:S(2)}) collective-permute-start(f32[1,128,256]{2,1,0:T(8,128)S(1)} %collective-permute-done.4), channel_id=1, source_target_pairs={{0,2},{2,4},{4,6},{6,8},{8,10},{10,12},{12,14},{14,16},{16,18},{18... | collective-permute-start | bytes 393224 | tf_op jit(solution)/shard_map/ppermute | solution.py:53
  46.0 7.2 %collective-permute-start.7 = (f32[1,128,256]{2,1,0:T(8,128)S(1)}, f32[1,128,256]{2,1,0:T(8,128)S(1)}, u32[]{:S(2)}, u32[]{:S(2)}) collective-permute-start(f32[1,128,256]{2,1,0:T(8,128)S(1)} %collective-permute-done.5), channel_id=1, source_target_pairs={{0,30},{2,0},{4,2},{6,4},{8,6},{10,8},{12,10},{14,12},{16,14},{18,... | collective-permute-start | bytes 393224 | tf_op jit(solution)/shard_map/ppermute | solution.py:60
  53.2 7.2 %collective-permute-start.8 = (f32[1,128,256]{2,1,0:T(8,128)S(1)}, f32[1,128,256]{2,1,0:T(8,128)S(1)}, u32[]{:S(2)}, u32[]{:S(2)}) collective-permute-start(f32[1,128,256]{2,1,0:T(8,128)S(1)} %collective-permute-done.6), channel_id=1, source_target_pairs={{0,2},{2,4},{4,6},{6,8},{8,10},{10,12},{12,14},{14,16},{16,18},{18... | collective-permute-start | bytes 393224 | tf_op jit(solution)/shard_map/ppermute | solution.py:53
  53.2 7.2 %collective-permute-start.9 = (f32[1,128,256]{2,1,0:T(8,128)S(1)}, f32[1,128,256]{2,1,0:T(8,128)S(1)}, u32[]{:S(2)}, u32[]{:S(2)}) collective-permute-start(f32[1,128,256]{2,1,0:T(8,128)S(1)} %collective-permute-done.7), channel_id=1, source_target_pairs={{0,30},{2,0},{4,2},{6,4},{8,6},{10,8},{12,10},{14,12},{16,14},{18,... | collective-permute-start | bytes 393224 | tf_op jit(solution)/shard_map/ppermute | solution.py:60
  60.4 7.2 %collective-permute-start.10 = (f32[1,128,256]{2,1,0:T(8,128)S(1)}, f32[1,128,256]{2,1,0:T(8,128)S(1)}, u32[]{:S(2)}, u32[]{:S(2)}) collective-permute-start(f32[1,128,256]{2,1,0:T(8,128)S(1)} %collective-permute-done.8), channel_id=1, source_target_pairs={{0,2},{2,4},{4,6},{6,8},{8,10},{10,12},{12,14},{14,16},{16,18},{18... | collective-permute-start | bytes 393224 | tf_op jit(solution)/shard_map/ppermute | solution.py:53
  60.4 7.2 %collective-permute-start.11 = (f32[1,128,256]{2,1,0:T(8,128)S(1)}, f32[1,128,256]{2,1,0:T(8,128)S(1)}, u32[]{:S(2)}, u32[]{:S(2)}) collective-permute-start(f32[1,128,256]{2,1,0:T(8,128)S(1)} %collective-permute-done.9), channel_id=1, source_target_pairs={{0,30},{2,0},{4,2},{6,4},{8,6},{10,8},{12,10},{14,12},{16,14},{18,... | collective-permute-start | bytes 393224 | tf_op jit(solution)/shard_map/ppermute | solution.py:60
  67.6 7.1 %collective-permute-start.13 = (f32[1,128,256]{2,1,0:T(8,128)S(1)}, f32[1,128,256]{2,1,0:T(8,128)S(1)}, u32[]{:S(2)}, u32[]{:S(2)}) collective-permute-start(f32[1,128,256]{2,1,0:T(8,128)S(1)} %collective-permute-done.11), channel_id=1, source_target_pairs={{0,30},{2,0},{4,2},{6,4},{8,6},{10,8},{12,10},{14,12},{16,14},{18,... | collective-permute-start | bytes 393224 | tf_op jit(solution)/shard_map/ppermute | solution.py:60
  101.4 93.8 %reduce-scatter.7.cloned.1.call-start = ((), (), s32[]{:S(2)}) async-start(), calls=%async_computation.5 | async-start | bytes 393216 | tf_op jit(solution)/shard_map/reduce_scatter | solution.py:31
  112.0 7.2 %collective-permute-start.15 = (f32[1,128,256]{2,1,0:T(8,128)S(1)}, f32[1,128,256]{2,1,0:T(8,128)S(1)}, u32[]{:S(2)}, u32[]{:S(2)}) collective-permute-start(f32[1,128,256]{2,1,0:T(8,128)S(1)} %bitcast.216), channel_id=1, source_target_pairs={{0,2},{2,4},{4,6},{6,8},{8,10},{10,12},{12,14},{14,16},{16,18},{18... | collective-permute-start | bytes 393224 | tf_op jit(solution)/shard_map/ppermute | solution.py:53
  112.2 7.1 %collective-permute-start.16 = (f32[1,128,256]{2,1,0:T(8,128)S(1)}, f32[1,128,256]{2,1,0:T(8,128)S(1)}, u32[]{:S(2)}, u32[]{:S(2)}) collective-permute-start(f32[1,128,256]{2,1,0:T(8,128)S(1)} %bitcast.217), channel_id=1, source_target_pairs={{0,30},{2,0},{4,2},{6,4},{8,6},{10,8},{12,10},{14,12},{16,14},{18,... | collective-permute-start | bytes 393224 | tf_op jit(solution)/shard_map/ppermute | solution.py:60
  126.4 7.2 %collective-permute-start.19 = (f32[1,128,256]{2,1,0:T(8,128)S(1)}, f32[1,128,256]{2,1,0:T(8,128)S(1)}, u32[]{:S(2)}, u32[]{:S(2)}) collective-permute-start(f32[1,128,256]{2,1,0:T(8,128)S(1)} %collective-permute-done.17), channel_id=1, source_target_pairs={{0,2},{2,4},{4,6},{6,8},{8,10},{10,12},{12,14},{14,16},{16,18},{18... | collective-permute-start | bytes 393224 | tf_op jit(solution)/shard_map/ppermute | solution.py:53
  126.4 7.2 %collective-permute-start.20 = (f32[1,128,256]{2,1,0:T(8,128)S(1)}, f32[1,128,256]{2,1,0:T(8,128)S(1)}, u32[]{:S(2)}, u32[]{:S(2)}) collective-permute-start(f32[1,128,256]{2,1,0:T(8,128)S(1)} %collective-permute-done.18), channel_id=1, source_target_pairs={{0,30},{2,0},{4,2},{6,4},{8,6},{10,8},{12,10},{14,12},{16,14},{18,... | collective-permute-start | bytes 393224 | tf_op jit(solution)/shard_map/ppermute | solution.py:60
  133.6 7.2 %collective-permute-start.21 = (f32[1,128,256]{2,1,0:T(8,128)S(1)}, f32[1,128,256]{2,1,0:T(8,128)S(1)}, u32[]{:S(2)}, u32[]{:S(2)}) collective-permute-start(f32[1,128,256]{2,1,0:T(8,128)S(1)} %collective-permute-done.19), channel_id=1, source_target_pairs={{0,2},{2,4},{4,6},{6,8},{8,10},{10,12},{12,14},{14,16},{16,18},{18... | collective-permute-start | bytes 393224 | tf_op jit(solution)/shard_map/ppermute | solution.py:53
  133.6 7.2 %collective-permute-start.22 = (f32[1,128,256]{2,1,0:T(8,128)S(1)}, f32[1,128,256]{2,1,0:T(8,128)S(1)}, u32[]{:S(2)}, u32[]{:S(2)}) collective-permute-start(f32[1,128,256]{2,1,0:T(8,128)S(1)} %collective-permute-done.20), channel_id=1, source_target_pairs={{0,30},{2,0},{4,2},{6,4},{8,6},{10,8},{12,10},{14,12},{16,14},{18,... | collective-permute-start | bytes 393224 | tf_op jit(solution)/shard_map/ppermute | solution.py:60
  140.8 7.2 %collective-permute-start.23 = (f32[1,128,256]{2,1,0:T(8,128)S(1)}, f32[1,128,256]{2,1,0:T(8,128)S(1)}, u32[]{:S(2)}, u32[]{:S(2)}) collective-permute-start(f32[1,128,256]{2,1,0:T(8,128)S(1)} %collective-permute-done.21), channel_id=1, source_target_pairs={{0,2},{2,4},{4,6},{6,8},{8,10},{10,12},{12,14},{14,16},{16,18},{18... | collective-permute-start | bytes 393224 | tf_op jit(solution)/shard_map/ppermute | solution.py:53
  140.8 7.2 %collective-permute-start.24 = (f32[1,128,256]{2,1,0:T(8,128)S(1)}, f32[1,128,256]{2,1,0:T(8,128)S(1)}, u32[]{:S(2)}, u32[]{:S(2)}) collective-permute-start(f32[1,128,256]{2,1,0:T(8,128)S(1)} %collective-permute-done.22), channel_id=1, source_target_pairs={{0,30},{2,0},{4,2},{6,4},{8,6},{10,8},{12,10},{14,12},{16,14},{18,... | collective-permute-start | bytes 393224 | tf_op jit(solution)/shard_map/ppermute | solution.py:60
  148.0 7.2 %collective-permute-start.25 = (f32[1,128,256]{2,1,0:T(8,128)S(1)}, f32[1,128,256]{2,1,0:T(8,128)S(1)}, u32[]{:S(2)}, u32[]{:S(2)}) collective-permute-start(f32[1,128,256]{2,1,0:T(8,128)S(1)} %collective-permute-done.23), channel_id=1, source_target_pairs={{0,2},{2,4},{4,6},{6,8},{8,10},{10,12},{12,14},{14,16},{16,18},{18... | collective-permute-start | bytes 393224 | tf_op jit(solution)/shard_map/ppermute | solution.py:53
  148.0 7.2 %collective-permute-start.26 = (f32[1,128,256]{2,1,0:T(8,128)S(1)}, f32[1,128,256]{2,1,0:T(8,128)S(1)}, u32[]{:S(2)}, u32[]{:S(2)}) collective-permute-start(f32[1,128,256]{2,1,0:T(8,128)S(1)} %collective-permute-done.24), channel_id=1, source_target_pairs={{0,30},{2,0},{4,2},{6,4},{8,6},{10,8},{12,10},{14,12},{16,14},{18,... | collective-permute-start | bytes 393224 | tf_op jit(solution)/shard_map/ppermute | solution.py:60
  187.3 92.0 %reduce-scatter.9.cloned.1.call-start = ((), (), s32[]{:S(2)}) async-start(), calls=%async_computation.6 | async-start | bytes 393216 | tf_op jit(solution)/shard_map/reduce_scatter | solution.py:31
  196.3 7.2 %collective-permute-start.30 = (f32[1,128,256]{2,1,0:T(8,128)S(1)}, f32[1,128,256]{2,1,0:T(8,128)S(1)}, u32[]{:S(2)}, u32[]{:S(2)}) collective-permute-start(f32[1,128,256]{2,1,0:T(8,128)S(1)} %bitcast.208), channel_id=1, source_target_pairs={{0,2},{2,4},{4,6},{6,8},{8,10},{10,12},{12,14},{14,16},{16,18},{18... | collective-permute-start | bytes 393224 | tf_op jit(solution)/shard_map/ppermute | solution.py:53
  196.4 7.2 %collective-permute-start.31 = (f32[1,128,256]{2,1,0:T(8,128)S(1)}, f32[1,128,256]{2,1,0:T(8,128)S(1)}, u32[]{:S(2)}, u32[]{:S(2)}) collective-permute-start(f32[1,128,256]{2,1,0:T(8,128)S(1)} %bitcast.209), channel_id=1, source_target_pairs={{0,30},{2,0},{4,2},{6,4},{8,6},{10,8},{12,10},{14,12},{16,14},{18,... | collective-permute-start | bytes 393224 | tf_op jit(solution)/shard_map/ppermute | solution.py:60
  210.7 7.2 %collective-permute-start.34 = (f32[1,128,256]{2,1,0:T(8,128)S(1)}, f32[1,128,256]{2,1,0:T(8,128)S(1)}, u32[]{:S(2)}, u32[]{:S(2)}) collective-permute-start(f32[1,128,256]{2,1,0:T(8,128)S(1)} %collective-permute-done.32), channel_id=1, source_target_pairs={{0,2},{2,4},{4,6},{6,8},{8,10},{10,12},{12,14},{14,16},{16,18},{18... | collective-permute-start | bytes 393224 | tf_op jit(solution)/shard_map/ppermute | solution.py:53
  210.7 7.2 %collective-permute-start.35 = (f32[1,128,256]{2,1,0:T(8,128)S(1)}, f32[1,128,256]{2,1,0:T(8,128)S(1)}, u32[]{:S(2)}, u32[]{:S(2)}) collective-permute-start(f32[1,128,256]{2,1,0:T(8,128)S(1)} %collective-permute-done.33), channel_id=1, source_target_pairs={{0,30},{2,0},{4,2},{6,4},{8,6},{10,8},{12,10},{14,12},{16,14},{18,... | collective-permute-start | bytes 393224 | tf_op jit(solution)/shard_map/ppermute | solution.py:60
  217.9 7.2 %collective-permute-start.36 = (f32[1,128,256]{2,1,0:T(8,128)S(1)}, f32[1,128,256]{2,1,0:T(8,128)S(1)}, u32[]{:S(2)}, u32[]{:S(2)}) collective-permute-start(f32[1,128,256]{2,1,0:T(8,128)S(1)} %collective-permute-done.34), channel_id=1, source_target_pairs={{0,2},{2,4},{4,6},{6,8},{8,10},{10,12},{12,14},{14,16},{16,18},{18... | collective-permute-start | bytes 393224 | tf_op jit(solution)/shard_map/ppermute | solution.py:53
  217.9 7.2 %collective-permute-start.37 = (f32[1,128,256]{2,1,0:T(8,128)S(1)}, f32[1,128,256]{2,1,0:T(8,128)S(1)}, u32[]{:S(2)}, u32[]{:S(2)}) collective-permute-start(f32[1,128,256]{2,1,0:T(8,128)S(1)} %collective-permute-done.35), channel_id=1, source_target_pairs={{0,30},{2,0},{4,2},{6,4},{8,6},{10,8},{12,10},{14,12},{16,14},{18,... | collective-permute-start | bytes 393224 | tf_op jit(solution)/shard_map/ppermute | solution.py:60
  225.1 7.2 %collective-permute-start.38 = (f32[1,128,256]{2,1,0:T(8,128)S(1)}, f32[1,128,256]{2,1,0:T(8,128)S(1)}, u32[]{:S(2)}, u32[]{:S(2)}) collective-permute-start(f32[1,128,256]{2,1,0:T(8,128)S(1)} %collective-permute-done.36), channel_id=1, source_target_pairs={{0,2},{2,4},{4,6},{6,8},{8,10},{10,12},{12,14},{14,16},{16,18},{18... | collective-permute-start | bytes 393224 | tf_op jit(solution)/shard_map/ppermute | solution.py:53
  225.1 7.2 %collective-permute-start.39 = (f32[1,128,256]{2,1,0:T(8,128)S(1)}, f32[1,128,256]{2,1,0:T(8,128)S(1)}, u32[]{:S(2)}, u32[]{:S(2)}) collective-permute-start(f32[1,128,256]{2,1,0:T(8,128)S(1)} %collective-permute-done.37), channel_id=1, source_target_pairs={{0,30},{2,0},{4,2},{6,4},{8,6},{10,8},{12,10},{14,12},{16,14},{18,... | collective-permute-start | bytes 393224 | tf_op jit(solution)/shard_map/ppermute | solution.py:60
  232.2 7.2 %collective-permute-start.40 = (f32[1,128,256]{2,1,0:T(8,128)S(1)}, f32[1,128,256]{2,1,0:T(8,128)S(1)}, u32[]{:S(2)}, u32[]{:S(2)}) collective-permute-start(f32[1,128,256]{2,1,0:T(8,128)S(1)} %collective-permute-done.38), channel_id=1, source_target_pairs={{0,2},{2,4},{4,6},{6,8},{8,10},{10,12},{12,14},{14,16},{16,18},{18... | collective-permute-start | bytes 393224 | tf_op jit(solution)/shard_map/ppermute | solution.py:53
  232.3 7.2 %collective-permute-start.41 = (f32[1,128,256]{2,1,0:T(8,128)S(1)}, f32[1,128,256]{2,1,0:T(8,128)S(1)}, u32[]{:S(2)}, u32[]{:S(2)}) collective-permute-start(f32[1,128,256]{2,1,0:T(8,128)S(1)} %collective-permute-done.39), channel_id=1, source_target_pairs={{0,30},{2,0},{4,2},{6,4},{8,6},{10,8},{12,10},{14,12},{16,14},{18,... | collective-permute-start | bytes 393224 | tf_op jit(solution)/shard_map/ppermute | solution.py:60
  271.4 92.2 %reduce-scatter.11.cloned.1.call-start = ((), (), s32[]{:S(2)}) async-start(), calls=%async_computation.7 | async-start | bytes 393216 | tf_op jit(solution)/shard_map/reduce_scatter | solution.py:31
  280.5 7.2 %collective-permute-start.45 = (f32[1,128,256]{2,1,0:T(8,128)S(1)}, f32[1,128,256]{2,1,0:T(8,128)S(1)}, u32[]{:S(2)}, u32[]{:S(2)}) collective-permute-start(f32[1,128,256]{2,1,0:T(8,128)S(1)} %bitcast.211), channel_id=1, source_target_pairs={{0,2},{2,4},{4,6},{6,8},{8,10},{10,12},{12,14},{14,16},{16,18},{18... | collective-permute-start | bytes 393224 | tf_op jit(solution)/shard_map/ppermute | solution.py:53
  280.6 7.1 %collective-permute-start.46 = (f32[1,128,256]{2,1,0:T(8,128)S(1)}, f32[1,128,256]{2,1,0:T(8,128)S(1)}, u32[]{:S(2)}, u32[]{:S(2)}) collective-permute-start(f32[1,128,256]{2,1,0:T(8,128)S(1)} %bitcast.212), channel_id=1, source_target_pairs={{0,30},{2,0},{4,2},{6,4},{8,6},{10,8},{12,10},{14,12},{16,14},{18,... | collective-permute-start | bytes 393224 | tf_op jit(solution)/shard_map/ppermute | solution.py:60
  294.8 7.2 %collective-permute-start.49 = (f32[1,128,256]{2,1,0:T(8,128)S(1)}, f32[1,128,256]{2,1,0:T(8,128)S(1)}, u32[]{:S(2)}, u32[]{:S(2)}) collective-permute-start(f32[1,128,256]{2,1,0:T(8,128)S(1)} %collective-permute-done.47), channel_id=1, source_target_pairs={{0,2},{2,4},{4,6},{6,8},{8,10},{10,12},{12,14},{14,16},{16,18},{18... | collective-permute-start | bytes 393224 | tf_op jit(solution)/shard_map/ppermute | solution.py:53
  294.9 7.2 %collective-permute-start.50 = (f32[1,128,256]{2,1,0:T(8,128)S(1)}, f32[1,128,256]{2,1,0:T(8,128)S(1)}, u32[]{:S(2)}, u32[]{:S(2)}) collective-permute-start(f32[1,128,256]{2,1,0:T(8,128)S(1)} %collective-permute-done.48), channel_id=1, source_target_pairs={{0,30},{2,0},{4,2},{6,4},{8,6},{10,8},{12,10},{14,12},{16,14},{18,... | collective-permute-start | bytes 393224 | tf_op jit(solution)/shard_map/ppermute | solution.py:60
  302.0 7.2 %collective-permute-start.51 = (f32[1,128,256]{2,1,0:T(8,128)S(1)}, f32[1,128,256]{2,1,0:T(8,128)S(1)}, u32[]{:S(2)}, u32[]{:S(2)}) collective-permute-start(f32[1,128,256]{2,1,0:T(8,128)S(1)} %collective-permute-done.49), channel_id=1, source_target_pairs={{0,2},{2,4},{4,6},{6,8},{8,10},{10,12},{12,14},{14,16},{16,18},{18... | collective-permute-start | bytes 393224 | tf_op jit(solution)/shard_map/ppermute | solution.py:53
  302.1 7.2 %collective-permute-start.52 = (f32[1,128,256]{2,1,0:T(8,128)S(1)}, f32[1,128,256]{2,1,0:T(8,128)S(1)}, u32[]{:S(2)}, u32[]{:S(2)}) collective-permute-start(f32[1,128,256]{2,1,0:T(8,128)S(1)} %collective-permute-done.50), channel_id=1, source_target_pairs={{0,30},{2,0},{4,2},{6,4},{8,6},{10,8},{12,10},{14,12},{16,14},{18,... | collective-permute-start | bytes 393224 | tf_op jit(solution)/shard_map/ppermute | solution.py:60
  309.2 7.2 %collective-permute-start.53 = (f32[1,128,256]{2,1,0:T(8,128)S(1)}, f32[1,128,256]{2,1,0:T(8,128)S(1)}, u32[]{:S(2)}, u32[]{:S(2)}) collective-permute-start(f32[1,128,256]{2,1,0:T(8,128)S(1)} %collective-permute-done.51), channel_id=1, source_target_pairs={{0,2},{2,4},{4,6},{6,8},{8,10},{10,12},{12,14},{14,16},{16,18},{18... | collective-permute-start | bytes 393224 | tf_op jit(solution)/shard_map/ppermute | solution.py:53
  309.2 7.2 %collective-permute-start.54 = (f32[1,128,256]{2,1,0:T(8,128)S(1)}, f32[1,128,256]{2,1,0:T(8,128)S(1)}, u32[]{:S(2)}, u32[]{:S(2)}) collective-permute-start(f32[1,128,256]{2,1,0:T(8,128)S(1)} %collective-permute-done.52), channel_id=1, source_target_pairs={{0,30},{2,0},{4,2},{6,4},{8,6},{10,8},{12,10},{14,12},{16,14},{18,... | collective-permute-start | bytes 393224 | tf_op jit(solution)/shard_map/ppermute | solution.py:60
  316.4 7.2 %collective-permute-start.55 = (f32[1,128,256]{2,1,0:T(8,128)S(1)}, f32[1,128,256]{2,1,0:T(8,128)S(1)}, u32[]{:S(2)}, u32[]{:S(2)}) collective-permute-start(f32[1,128,256]{2,1,0:T(8,128)S(1)} %collective-permute-done.53), channel_id=1, source_target_pairs={{0,2},{2,4},{4,6},{6,8},{8,10},{10,12},{12,14},{14,16},{16,18},{18... | collective-permute-start | bytes 393224 | tf_op jit(solution)/shard_map/ppermute | solution.py:53
  316.4 7.2 %collective-permute-start.56 = (f32[1,128,256]{2,1,0:T(8,128)S(1)}, f32[1,128,256]{2,1,0:T(8,128)S(1)}, u32[]{:S(2)}, u32[]{:S(2)}) collective-permute-start(f32[1,128,256]{2,1,0:T(8,128)S(1)} %collective-permute-done.54), channel_id=1, source_target_pairs={{0,30},{2,0},{4,2},{6,4},{8,6},{10,8},{12,10},{14,12},{16,14},{18,... | collective-permute-start | bytes 393224 | tf_op jit(solution)/shard_map/ppermute | solution.py:60
  323.7 7.2 %collective-permute-start.58 = (f32[1,128,256]{2,1,0:T(8,128)S(1)}, f32[1,128,256]{2,1,0:T(8,128)S(1)}, u32[]{:S(2)}, u32[]{:S(2)}) collective-permute-start(f32[1,128,256]{2,1,0:T(8,128)S(1)} %collective-permute-done.56), channel_id=1, source_target_pairs={{0,30},{2,0},{4,2},{6,4},{8,6},{10,8},{12,10},{14,12},{16,14},{18,... | collective-permute-start | bytes 393224 | tf_op jit(solution)/shard_map/ppermute | solution.py:60
  (23 other events, 156.9 us)
Sparse Core Ops, SparseCore 0:
  101.5 9.3 reduce-scatter.4
  187.4 7.7 reduce-scatter.6
  271.5 7.7 reduce-scatter.8
  355.9 7.7 reduce-scatter.10
